TPU v7x, 256 devices: a whole 4x4x8 slice. The times are simulated.
256 devices in a mesh: inst: 4 (over x_lo, core), space: 64 (over x_hi, z, y).
Axes of the slice: x: 4 (x_hi: 2, x_lo: 2; x = x_hi * 2 + x_lo), y: 4, z: 8, core: 2. Of those that a mesh axis runs over, the one named last changes fastest.
Arguments:
- flow_state: float32 [8, 5, 4096, 256], P('inst', None, 'space'), may hold values from -6 to 6
- flow_source: float32 [8, 5, 4096, 256], P('inst', None, 'space'), may hold values from -6 to 6
- pseudo_step: float32 [4096, 256], P('space'), may hold values from 0.03 to 0.12
- flux_jacobian: float32 [5, 5], replicated, may hold values from -2.5 to 2.5
- stator_donor: int32 [8, 4096], P('inst', 'space'), may hold values from 0 to 4095, as said below
- stator_weight: float32 [8, 4096], P('inst', 'space'), may hold values from 0 to 1
- rotor_donor: int32 [8, 4096], P('inst', 'space'), may hold values from 0 to 4095, as said below
- rotor_weight: float32 [8, 4096], P('inst', 'space'), may hold values from 0 to 1
Outputs:
- new_state: float32 [8, 5, 4096, 256], P('inst', None, 'space')
- residual: float32 [8, 5, 4096, 256], P('inst', None, 'space')
Inputs may be any that keep to these rules, and one draw needn't show every extreme that they name: `stator_donor`: for each instance n the row holds the rotation j -> (j - shift_n) mod 4096 of the rows, so entry j is (j - stator_shift_n) mod 4096, where stator_shift_n is a shift of its own for each instance. `rotor_donor`: for each instance n the row holds the rotation j -> (j + shift_n) mod 4096 of the rows, so entry j is (j + rotor_shift_n) mod 4096, where rotor_shift_n is a shift of its own for each instance, independent of stator_shift_n.
All inputs are finite; a program needn't handle non-finite values.
Results may differ from a plain program's by a relative error of at most 0.0001.
Values sent between devices are 32-bit elements; how exact they have to be, the bound alone decides.
A program may use at most 128 MiB of HBM per device.

v0:
```python
import math
import jax
import jax.numpy as jnp
from jax import lax
from jax.sharding import PartitionSpec as P

NT = 8
SWEEPS = 2
viscosity = 0.5


def with_halo(x, sides, width):
    for axis, dim in sides:
        count, length = (lax.axis_size(axis), x.shape[dim])
        up = [(i, (i + 1) % count) for i in range(count)]
        down = [(j, i) for i, j in up]
        last = lax.slice_in_dim(x, length - width, length, axis=dim)
        leading = lax.slice_in_dim(x, 0, width, axis=dim)
        before = lax.ppermute(last, axis, up)
        after = lax.ppermute(leading, axis, down)
        x = jnp.concatenate([before, x, after], axis=dim)
    return x


def spectral_table(count):
    rows = jnp.arange(count, dtype=jnp.int32)[:, None]
    columns = jnp.arange(count, dtype=jnp.int32)[None, :]
    gap = rows - columns
    parity = (1 - 2 * (gap % 2)).astype(jnp.float32)
    angle = math.pi / count * gap.astype(jnp.float32)
    sine = jnp.where(gap == 0, jnp.float32(1.0), jnp.sin(angle))
    value = 0.5 * parity * jnp.cos(angle) / sine
    return jnp.where(gap == 0, jnp.float32(0.0), value)


def interpolate(column, donor, weight):
    total = column.shape[2]
    first = jnp.take_along_axis(column, donor[:, None, :], axis=2)
    second = jnp.take_along_axis(column, ((donor + 1) % total)[:, None, :], axis=2)
    return (1.0 - weight)[:, None, :] * first + weight[:, None, :] * second


def spatial(flow, upper, lower, stator_in, rotor_in, flux_jacobian):
    half = flow.shape[3] // 2
    zero_col = jnp.zeros(flow.shape[:3] + (1,), jnp.float32)
    left_cells = jnp.concatenate([zero_col, flow[..., :-1]], axis=3).at[..., half].set(stator_in)
    right_cells = jnp.concatenate([flow[..., 1:], zero_col], axis=3).at[..., half - 1].set(rotor_in)
    convect = jnp.einsum(
        "vw,nwca->nvca", flux_jacobian, flow - left_cells, precision=lax.Precision.HIGHEST
    )
    return convect + viscosity * (4.0 * flow - left_cells - right_cells - upper - lower)


def apply_columns(local_rows, piece):
    return jnp.einsum("nm,mvca->nvca", local_rows, piece, precision=lax.Precision.HIGHEST)


def local(
    flow_state,
    flow_source,
    pseudo_step,
    flux_jacobian,
    stator_donor,
    stator_weight,
    rotor_donor,
    rotor_weight,
):
    local_count = flow_state.shape[0]
    position = lax.axis_index("inst")
    table = spectral_table(NT)
    half = flow_state.shape[3] // 2
    local_rows = lax.dynamic_slice_in_dim(table, position * local_count, local_count, 0)
    flow = flow_state
    residual = flow
    for sweep in range(SWEEPS):
        rotor_all, stator_all = (
            lax.all_gather(flow[..., half - 1], "space", axis=2, tiled=True),
            lax.all_gather(flow[..., half], "space", axis=2, tiled=True),
        )
        stator_in = interpolate(rotor_all, stator_donor, stator_weight)
        rotor_in = interpolate(stator_all, rotor_donor, rotor_weight)
        padded = with_halo(flow, (("space", 2),), 1)
        upper = padded[:, :, :-2]
        lower = padded[:, :, 2:]
        derivative = apply_columns(local_rows, lax.all_gather(flow, "inst", axis=0, tiled=True))
        residual = (
            spatial(flow, upper, lower, stator_in, rotor_in, flux_jacobian)
            + derivative
            - flow_source
        )
        flow = flow - pseudo_step[None, None] * residual
    return (flow, residual)


def solution(mesh):
    return jax.shard_map(
        local,
        mesh=mesh,
        in_specs=(
            P("inst", None, "space", None),
            P("inst", None, "space", None),
            P("space", None),
            P(),
            P("inst", "space"),
            P("inst", "space"),
            P("inst", "space"),
            P("inst", "space"),
        ),
        out_specs=(P("inst", None, "space", None), P("inst", None, "space", None)),
        check_vma=False,
    )
```

profile of v0, /device:TPU:6, one launch (start us, length us, event | category | flops | bytes accessed | tf_op | source)
XLA Modules:
  0.0 1462.7 jit_solution(14926466707886030366)
XLA Ops:
  7.2 0.0 copy-start
  7.2 0.0 all-gather.7.cloned.1.call-start
  7.2 0.7 all-gather.7.cloned.1.call-update
  7.9 0.0 all-gather.9.cloned.1.call-start
  8.0 1.5 copy.116
  9.5 1.7 collective-permute-start
  11.2 7.7 collective-permute-start.1
  18.8 1.2 fusion.59
  20.0 0.9 copy.137
  20.9 0.7 bitcast_or_fusion.3
  21.6 0.1 reshape.275
  21.7 212.1 %all-gather = f32[2,5,4096,1]{1,2,0,3:T(8,128)} all-gather(f32[2,5,64,1]{1,2,0,3:T(8,128)S(1)} %copy.137), channel_id=2, replica_groups=mesh['inst'=4,'space'=64] {'space'}, dimensions={2}, use_global_device_ids=true | all-gather | bytes 166400 | tf_op jit(solution)/shard_map/all_gather | solution.py:77
  233.8 1.8 gather_fusion.1
  235.5 0.1 copy.100
  235.6 0.1 reshape.270
  235.7 1.8 gather_fusion
  237.5 0.1 copy.99
  237.6 0.3 copy.101
  237.9 0.9 copy.138
  238.8 0.1 reshape.280
  238.9 209.7 %all-gather.1 = f32[2,5,4096,1]{1,2,0,3:T(8,128)} all-gather(f32[2,5,64,1]{1,2,0,3:T(8,128)S(1)} %copy.138), channel_id=3, replica_groups=mesh['inst'=4,'space'=64] {'space'}, dimensions={2}, use_global_device_ids=true | all-gather | bytes 166400 | tf_op jit(solution)/shard_map/all_gather | solution.py:78
  448.6 1.8 gather_fusion.2
  450.3 0.1 copy.106
  450.4 0.1 reshape.285
  450.5 1.8 gather_fusion.3
  452.3 0.1 copy.107
  452.4 1.0 copy.108
  453.5 0.3 fusion.57
  453.8 0.3 concatenate.34
  454.2 1.0 concatenate.35
  455.2 1.8 scatter.14
  457.0 12.3 scatter.15
  469.4 0.0 all-gather.7.cloned.1.call-done
  469.4 5.3 fusion.2
  474.8 3.9 fusion.5
  478.7 1.0 copy.129
  479.7 0.0 all-gather.9.cloned.1.call-update
  479.7 0.2 fusion.54
  479.9 453.1 %all-gather.2 = f32[2,5,4096,1]{3,1,2,0:T(8,128)} all-gather(f32[2,5,64,1]{3,1,2,0:T(8,128)S(1)} %get-tuple-element.59), channel_id=4, replica_groups=mesh['inst'=4,'space'=64] {'space'}, dimensions={2}, use_global_device_ids=true | all-gather | bytes 166400 | tf_op jit(solution)/shard_map/all_gather | solution.py:77
  933.0 17.8 %copy.117 = f32[2,5,4096,1]{2,0,1,3:T(2,128)S(1)} copy(f32[2,5,4096,1]{3,1,2,0:T(8,128)} %all-gather.2) | data formatting | bytes 327680 | tf_op jit(solution)/shard_map/all_gather | solution.py:77
  950.8 2.7 copy.118
  953.5 1.8 gather_fusion.4
  955.3 1.8 gather_fusion.5
  957.0 436.0 %all-gather.3 = f32[2,5,4096,1]{3,1,2,0:T(8,128)} all-gather(f32[2,5,64,1]{3,1,2,0:T(8,128)S(1)} %get-tuple-element.60), channel_id=5, replica_groups=mesh['inst'=4,'space'=64] {'space'}, dimensions={2}, use_global_device_ids=true | all-gather | bytes 166400 | tf_op jit(solution)/shard_map/all_gather | solution.py:78
  1393.1 17.8 %copy.123 = f32[2,5,4096,1]{2,0,1,3:T(2,128)S(1)} copy(f32[2,5,4096,1]{3,1,2,0:T(8,128)} %all-gather.3) | data formatting | bytes 327680 | tf_op jit(solution)/shard_map/all_gather | solution.py:78
  1410.8 2.7 copy.124
  1413.5 1.8 gather_fusion.6
  1415.3 1.8 gather_fusion.7
  1417.1 0.1 copy.119
  1417.1 0.1 copy.121
  1417.3 0.3 copy.122
  1417.5 1.3 fusion.55
  1418.8 0.3 concatenate.38
  1419.2 0.1 copy.125
  1419.3 0.1 copy.127
  1419.4 1.0 copy.128
  1420.4 2.3 concatenate.39
  1422.7 7.7 collective-permute-start.3
  1430.4 1.8 scatter.16
  1432.2 12.3 scatter.19
  1444.6 5.3 fusion
  1449.9 3.9 multiply_subtract_fusion
  1453.8 1.0 copy.133
  1454.8 1.0 copy.134
  (35 shorter events, 0.2 us)
Async XLA Ops:
  7.2 467.6 %copy-start = (f32[5,5]{1,0:T(8,128)S(1)}, f32[5,5]{1,0:T(8,128)}, u32[]{:S(2)}) copy-start(f32[5,5]{1,0:T(8,128)} %param.21) | copy-start | bytes 304
  7.2 462.2 %all-gather.7.cloned.1.call-start = ((), (), s32[]{:S(2)}) async-start(), calls=%async_computation | async-start | bytes 3276800 | tf_op jit(solution)/shard_map/all_gather | solution.py:85
  7.9 229.6 %copy-start.7 = (s32[2,64]{1,0:T(2,128)S(1)}, s32[2,64]{1,0:T(2,128)}, u32[]{:S(2)}) copy-start(s32[2,64]{1,0:T(2,128)} %param.22) | copy-start | bytes 1540
  7.9 229.7 %copy-start.5 = (f32[2,64]{1,0:T(2,128)S(1)}, f32[2,64]{1,0:T(2,128)}, u32[]{:S(2)}) copy-start(f32[2,64]{1,0:T(2,128)} %param.23) | copy-start | bytes 1540
  7.9 230.8 %copy-start.8 = (s32[2,64]{1,0:T(2,128)S(1)}, s32[2,64]{1,0:T(2,128)}, u32[]{:S(2)}) copy-start(s32[2,64]{1,0:T(2,128)} %param.24) | copy-start | bytes 1540
  7.9 1436.6 %all-gather.9.cloned.1.call-start = ((), (), s32[]{:S(2)}) async-start(), calls=%async_computation.1 | async-start | bytes 3276800 | tf_op jit(solution)/shard_map/all_gather | solution.py:85
  9.5 465.2 %collective-permute-start = (f32[2,5,1,256]{3,1,2,0:T(8,128)S(1)}, f32[2,5,1,256]{3,1,2,0:T(8,128)S(1)}, u32[]{:S(2)}, u32[]{:S(2)}) collective-permute-start(f32[2,5,1,256]{3,1,2,0:T(8,128)S(1)} %get-tuple-element.67), channel_id=1, source_target_pairs={{0,1},{1,2},{2,3},{3,4},{4,5},{5,6},{6,7},{7,8},{8,9},{9,10},{10,1... | collective-permute-start | bytes 30728 | tf_op jit(solution)/shard_map/ppermute | solution.py:19
  11.2 463.6 %collective-permute-start.1 = (f32[2,5,1,256]{3,1,2,0:T(8,128)S(1)}, f32[2,5,1,256]{3,1,2,0:T(8,128)S(1)}, u32[]{:S(2)}, u32[]{:S(2)}) collective-permute-start(f32[2,5,1,256]{3,1,2,0:T(8,128)S(1)} %get-tuple-element.68), channel_id=1, source_target_pairs={{1,0},{2,1},{3,2},{4,3},{5,4},{6,5},{7,6},{8,7},{9,8},{10,9},{11,1... | collective-permute-start | bytes 30728 | tf_op jit(solution)/shard_map/ppermute | solution.py:20
  21.7 430.7 %copy-start.6 = (f32[2,64]{1,0:T(2,128)S(1)}, f32[2,64]{1,0:T(2,128)}, u32[]{:S(2)}) copy-start(f32[2,64]{1,0:T(2,128)} %param.25) | copy-start | bytes 1540
  454.2 20.6 %copy-start.1 = (f32[2,5,64,256]{3,2,1,0:T(8,128)S(1)}, f32[2,5,64,256]{3,2,1,0:T(8,128)}, u32[]{:S(2)}) copy-start(f32[2,5,64,256]{3,2,1,0:T(8,128)} %param.19) | copy-start | bytes 1966084
  454.2 20.6 %copy-start.4 = (f32[64,256]{1,0:T(8,128)S(1)}, f32[64,256]{1,0:T(8,128)}, u32[]{:S(2)}) copy-start(f32[64,256]{1,0:T(8,128)} %param.20) | copy-start | bytes 196612
  457.0 17.7 %copy-start.3 = (f32[2,5,64,256]{3,1,2,0:T(8,128)}, f32[2,5,64,256]{3,1,2,0:T(8,128)S(1)}, u32[]{:S(2)}) copy-start(f32[2,5,64,256]{3,1,2,0:T(8,128)S(1)} %scatter.14) | copy-start | bytes 1966084
  1422.7 27.2 %collective-permute-start.2 = (f32[2,5,1,256]{3,1,2,0:T(8,128)S(1)}, f32[2,5,1,256]{3,1,2,0:T(8,128)S(1)}, u32[]{:S(2)}, u32[]{:S(2)}) collective-permute-start(f32[2,5,1,256]{3,1,2,0:T(8,128)S(1)} %get-tuple-element.63), channel_id=1, source_target_pairs={{0,1},{1,2},{2,3},{3,4},{4,5},{5,6},{6,7},{7,8},{8,9},{9,10},{10,1... | collective-permute-start | bytes 30728 | tf_op jit(solution)/shard_map/ppermute | solution.py:19
  1422.7 27.2 %collective-permute-start.3 = (f32[2,5,1,256]{3,1,2,0:T(8,128)S(1)}, f32[2,5,1,256]{3,1,2,0:T(8,128)S(1)}, u32[]{:S(2)}, u32[]{:S(2)}) collective-permute-start(f32[2,5,1,256]{3,1,2,0:T(8,128)S(1)} %get-tuple-element.64), channel_id=1, source_target_pairs={{1,0},{2,1},{3,2},{4,3},{5,4},{6,5},{7,6},{8,7},{9,8},{10,9},{11,1... | collective-permute-start | bytes 30728 | tf_op jit(solution)/shard_map/ppermute | solution.py:20
  1432.2 12.3 copy-start.2
Sparse Core Ops, SparseCore 0:
  9.8 38.0 all-gather.6
  479.9 29.6 all-gather.8
where the time goes:
time: 1460 us
  blocking collectives  1310 us (90%)
  local copies, waits for them, and re-layouts  100 us (7%)
  matrix products  18.4 us (1%)
  starting transfers between devices  17.1 us (1%)
    all_gather x2, blocking collectives, local(): lax.all_gather(flow[..., half - 1], 'space', axis=2, tiled=True)  665 us
    all_gather x2, blocking collectives, local(): lax.all_gather(flow[..., half], 'space', axis=2, tiled=True)  646 us
  transfers between devices with their start and end apart: 6, of which 0 were waited for; matrix products, arithmetic and copies ran while one was open for 7% of the time, Pallas kernels for 0%

commit v1 on v0

--- a/solution.py
+++ b/solution.py
@@ -75,7 +75,12 @@
     for sweep in range(SWEEPS):
         rotor_all, stator_all = (
             lax.all_gather(flow[..., half - 1], "space", axis=2, tiled=True),
-            lax.all_gather(flow[..., half], "space", axis=2, tiled=True),
+            jnp.concatenate(
+                lax.all_to_all(
+                    jnp.stack([flow[..., half]] * lax.axis_size("space")), "space", 0, 0
+                ),
+                axis=2,
+            ),
         )
         stator_in = interpolate(rotor_all, stator_donor, stator_weight)
         rotor_in = interpolate(stator_all, rotor_donor, rotor_weight)

time: 1460 us -> 827 us (0.57)
  blocking collectives: 1310 us -> 667 us
  starting transfers between devices: 17.1 us -> 35.8 us
    all_gather x2 -> x0, blocking collectives: 646 us -> none  [local(): lax.all_gather(flow[..., half], 'space', axis=2, tiled=True)]
    all_gather x2 -> x0, local copies, waits for them, and re-layouts: 20.5 us -> none  [local(): lax.all_gather(flow[..., half], 'space', axis=2, tiled=True)]
    all_to_all x0 -> x2, starting transfers between devices: none -> 20.2 us  [local(): lax.all_to_all(jnp.stack([flow[..., half]] * lax.axis_size('space')), 'sp...]
  transfers between devices with their start and end apart: 6 -> 8, of which waited for: 0 -> 0; matrix products, arithmetic and copies ran while one was open for 7% -> 12% of each run, Pallas kernels for 0% -> 0%
where the time goes in v1:
time: 827 us
  blocking collectives  667 us (81%)
  local copies, waits for them, and re-layouts  87.1 us (11%)
  starting transfers between devices  35.8 us (4%)
  matrix products  18.9 us (2%)
  between operations  14.5 us (2%)
    all_gather x2, blocking collectives, local(): lax.all_gather(flow[..., half - 1], 'space', axis=2, tiled=True)  667 us
    scatter x2, local copies, waits for them, and re-layouts, spatial(): jnp.concatenate([flow[..., 1:], zero_col], axis=3).at[..., half - 1]  20.8 us
    all_gather x2, local copies, waits for them, and re-layouts, local(): lax.all_gather(flow[..., half - 1], 'space', axis=2, tiled=True)  20.5 us
    all_to_all x2, starting transfers between devices, local(): lax.all_to_all(jnp.stack([flow[..., half]] * lax.axis_size('space')), 'sp...  20.2 us
  transfers between devices with their start and end apart: 8, of which 0 were waited for; matrix products, arithmetic and copies ran while one was open for 12% of the time, Pallas kernels for 0%

profile of v1, /device:TPU:6, one launch (start us, length us, event | category | flops | bytes accessed | tf_op | source)
XLA Modules:
  0.0 826.7 jit_solution(7323085985488087305)
XLA Ops:
  7.2 0.7 all-gather.5.cloned.1.call-update
  7.9 1.2 fusion.59
  9.2 0.1 copy.105
  9.3 0.1 broadcast_bitcast_fusion.1
  9.4 1.0 reshape.329
  10.4 14.7 %all-to-all-start = ((f32[64,1,640]{2,1,0:T(1,128)}), f32[64,1,640]{2,1,0:T(1,128)S(1)}, u32[]{:S(2)}, u32[]{:S(2)}) async-start(f32[64,1,640]{2,1,0:T(1,128)} %reshape.329), calls=%async_computation | async-start | bytes 327680 | tf_op jit(solution)/shard_map/all_to_all | solution.py:79
  25.2 1.5 copy.117
  26.8 1.5 collective-permute-start
  28.3 6.3 collective-permute-start.1
  34.6 0.1 reshape.298
  34.7 0.1 reshape.303
  34.8 0.9 copy.137
  35.7 0.1 reshape.293
  35.7 208.8 %all-gather = f32[2,5,4096,1]{1,2,0,3:T(8,128)} all-gather(f32[2,5,64,1]{1,2,0,3:T(8,128)S(1)} %copy.137), channel_id=2, replica_groups=mesh['inst'=4,'space'=64] {'space'}, dimensions={2}, use_global_device_ids=true | all-gather | bytes 166400 | tf_op jit(solution)/shard_map/all_gather | solution.py:77
  244.5 1.8 gather_fusion.1
  246.4 1.8 gather_fusion
  248.4 0.3 copy.101
  248.7 0.3 fusion.57
  249.1 1.3 concatenate.34
  250.4 3.0 scatter.14
  253.6 0.6 broadcast.403
  254.2 1.1 reduce.8
  255.3 0.2 reshape.330
  255.6 2.8 copy.106
  258.3 1.8 gather_fusion.2
  260.2 1.8 gather_fusion.3
  262.1 0.3 copy.109
  262.3 10.4 %scatter.15 = f32[2,5,64,256]{3,1,2,0:T(8,128)S(1)} dynamic-update-slice(f32[2,5,64,256]{3,1,2,0:T(8,128)S(1)} %concatenate.35, f32[2,5,64,1]{3,1,2,0:T(8,128)S(1)} %copy.109, s32[]{:T(128)} %constant.160.clone.1, s32[]{:T(128)} %constant.160.clone.1, s32[]{:T(128)} %constant.160.clone.1, s32[]{:T(128)} %constant.165.clone.1) | dynamic-update-slice | bytes 5124 | tf_op jit(solution)/shard_map/scatter | solution.py:47
  272.8 5.6 fusion.2
  278.5 4.0 fusion.5
  282.5 1.0 copy.129
  283.5 0.2 fusion.54
  283.7 457.8 %all-gather.1 = f32[2,5,4096,1]{3,1,2,0:T(8,128)} all-gather(f32[2,5,64,1]{3,1,2,0:T(8,128)S(1)} %get-tuple-element.59), channel_id=3, replica_groups=mesh['inst'=4,'space'=64] {'space'}, dimensions={2}, use_global_device_ids=true | all-gather | bytes 166400 | tf_op jit(solution)/shard_map/all_gather | solution.py:77
  741.5 17.8 %copy.118 = f32[2,5,4096,1]{2,0,1,3:T(2,128)S(1)} copy(f32[2,5,4096,1]{3,1,2,0:T(8,128)} %all-gather.1) | data formatting | bytes 327680 | tf_op jit(solution)/shard_map/all_gather | solution.py:77
  759.3 2.7 copy.119
  762.0 1.8 gather_fusion.4
  763.8 1.8 gather_fusion.5
  765.7 0.1 copy.122
  765.8 0.2 copy.124
  766.0 0.1 broadcast_bitcast_fusion
  766.1 1.0 reshape.331
  767.1 5.5 all-to-all-start.1
  772.5 1.3 fusion.55
  773.9 0.3 copy.123
  774.2 1.4 concatenate.38
  775.5 1.3 concatenate.39
  776.9 0.6 fusion.56
  777.5 1.5 collective-permute-start.2
  778.9 6.3 collective-permute-start.3
  785.2 3.0 scatter.16
  788.2 1.1 reduce.9
  789.3 0.2 reshape.332
  789.6 2.8 copy.125
  792.3 1.8 gather_fusion.6
  794.1 1.8 gather_fusion.7
  796.0 0.1 copy.127
  796.1 0.7 fusion.23
  796.8 0.3 copy.128
  797.0 10.4 %scatter.19 = f32[2,5,64,256]{3,1,2,0:T(8,128)S(1)} dynamic-update-slice(f32[2,5,64,256]{3,1,2,0:T(8,128)S(1)} %concatenate.39, f32[2,5,64,1]{3,1,2,0:T(8,128)S(1)} %copy.128, s32[]{:T(128)} %constant.160.clone.1, s32[]{:T(128)} %constant.160.clone.1, s32[]{:T(128)} %constant.160.clone.1, s32[]{:T(128)} %constant.165.clone.1) | dynamic-update-slice | bytes 5124 | tf_op jit(solution)/shard_map/scatter | solution.py:47
  807.4 1.0 copy-done.2
  808.4 5.3 fusion
  813.7 4.0 multiply_subtract_fusion
  817.8 1.0 copy.133
  818.8 1.0 copy.134
  (61 shorter events, 1.1 us)
Async XLA Ops:
  7.2 271.3 %copy-start = (f32[5,5]{1,0:T(8,128)S(1)}, f32[5,5]{1,0:T(8,128)}, u32[]{:S(2)}) copy-start(f32[5,5]{1,0:T(8,128)} %param.21) | copy-start | bytes 304
  7.2 27.4 %copy-start.14 = (s32[2,64]{1,0:T(2,128)S(1)}, s32[2,64]{1,0:T(2,128)}, u32[]{:S(2)}) copy-start(s32[2,64]{1,0:T(2,128)} %param.24) | copy-start | bytes 1540
  7.2 28.4 %copy-start.13 = (s32[2,64]{1,0:T(2,128)S(1)}, s32[2,64]{1,0:T(2,128)}, u32[]{:S(2)}) copy-start(s32[2,64]{1,0:T(2,128)} %param.22) | copy-start | bytes 1540
  7.2 265.6 %all-gather.5.cloned.1.call-start = ((), (), s32[]{:S(2)}) async-start(), calls=%async_computation.2 | async-start | bytes 3276800 | tf_op jit(solution)/shard_map/all_gather | solution.py:90
  9.2 239.2 %copy-start.5 = (f32[2,64]{1,0:T(2,128)S(1)}, f32[2,64]{1,0:T(2,128)}, u32[]{:S(2)}) copy-start(f32[2,64]{1,0:T(2,128)} %param.23) | copy-start | bytes 1540
  10.4 243.1 %all-to-all-start = ((f32[64,1,640]{2,1,0:T(1,128)}), f32[64,1,640]{2,1,0:T(1,128)S(1)}, u32[]{:S(2)}, u32[]{:S(2)}) async-start(f32[64,1,640]{2,1,0:T(1,128)} %reshape.329), calls=%async_computation | async-start | bytes 327680 | tf_op jit(solution)/shard_map/all_to_all | solution.py:79
  25.2 783.3 %all-gather.7.cloned.1.call-start = ((), (), s32[]{:S(2)}) async-start(), calls=%async_computation.3 | async-start | bytes 3276800 | tf_op jit(solution)/shard_map/all_gather | solution.py:90
  26.8 251.7 %collective-permute-start = (f32[2,5,1,256]{3,1,2,0:T(8,128)S(1)}, f32[2,5,1,256]{3,1,2,0:T(8,128)S(1)}, u32[]{:S(2)}, u32[]{:S(2)}) collective-permute-start(f32[2,5,1,256]{3,1,2,0:T(8,128)S(1)} %get-tuple-element.67), channel_id=1, source_target_pairs={{0,1},{1,2},{2,3},{3,4},{4,5},{5,6},{6,7},{7,8},{8,9},{9,10},{10,1... | collective-permute-start | bytes 30728 | tf_op jit(solution)/shard_map/ppermute | solution.py:19
  28.3 250.2 %collective-permute-start.1 = (f32[2,5,1,256]{3,1,2,0:T(8,128)S(1)}, f32[2,5,1,256]{3,1,2,0:T(8,128)S(1)}, u32[]{:S(2)}, u32[]{:S(2)}) collective-permute-start(f32[2,5,1,256]{3,1,2,0:T(8,128)S(1)} %get-tuple-element.68), channel_id=1, source_target_pairs={{1,0},{2,1},{3,2},{4,3},{5,4},{6,5},{7,6},{8,7},{9,8},{10,9},{11,1... | collective-permute-start | bytes 30728 | tf_op jit(solution)/shard_map/ppermute | solution.py:20
  248.3 2.1 copy-start.9
  248.4 2.1 copy-start.11
  248.7 4.9 copy-start.6
  253.5 25.0 %copy-start.7 = (pred[2,64]{1,0:T(4,128)(4,1)}, pred[2,64]{1,0:T(4,128)(4,1)S(1)}, u32[]{:S(2)}) copy-start(pred[2,64]{1,0:T(4,128)(4,1)S(1)} %get-tuple-element.75) | copy-start | bytes 388
  253.5 25.0 %copy-start.8 = (pred[2,64]{1,0:T(4,128)(4,1)}, pred[2,64]{1,0:T(4,128)(4,1)S(1)}, u32[]{:S(2)}) copy-start(pred[2,64]{1,0:T(4,128)(4,1)S(1)} %get-tuple-element.76) | copy-start | bytes 388
  255.5 23.0 %copy-start.1 = (f32[2,5,64,256]{3,2,1,0:T(8,128)S(1)}, f32[2,5,64,256]{3,2,1,0:T(8,128)}, u32[]{:S(2)}) copy-start(f32[2,5,64,256]{3,2,1,0:T(8,128)} %param.19) | copy-start | bytes 1966084
  255.6 23.0 %copy-start.4 = (f32[64,256]{1,0:T(8,128)S(1)}, f32[64,256]{1,0:T(8,128)}, u32[]{:S(2)}) copy-start(f32[64,256]{1,0:T(8,128)} %param.20) | copy-start | bytes 196612
  272.8 5.7 copy-start.3
  762.0 11.9 %copy-start.10 = (pred[2,64]{1,0:T(4,128)(4,1)S(1)}, pred[2,64]{1,0:T(4,128)(4,1)}, u32[]{:S(2)}) copy-start(pred[2,64]{1,0:T(4,128)(4,1)} %copy-done.9) | copy-start | bytes 388
  762.0 11.9 %copy-start.12 = (pred[2,64]{1,0:T(4,128)(4,1)S(1)}, pred[2,64]{1,0:T(4,128)(4,1)}, u32[]{:S(2)}) copy-start(pred[2,64]{1,0:T(4,128)(4,1)} %copy-done.11) | copy-start | bytes 388
  767.1 21.1 %all-to-all-start.1 = ((f32[64,1,640]{2,1,0:T(1,128)}), f32[64,1,640]{2,1,0:T(1,128)S(1)}, u32[]{:S(2)}, u32[]{:S(2)}) async-start(f32[64,1,640]{2,1,0:T(1,128)} %reshape.331), calls=%async_computation.1 | async-start | bytes 327680 | tf_op jit(solution)/shard_map/all_to_all | solution.py:79
  777.5 36.2 %collective-permute-start.2 = (f32[2,5,1,256]{3,1,2,0:T(8,128)}, f32[2,5,1,256]{3,1,2,0:T(8,128)S(1)}, u32[]{:S(2)}, u32[]{:S(2)}) collective-permute-start(f32[2,5,1,256]{3,1,2,0:T(8,128)} %get-tuple-element.63), channel_id=1, source_target_pairs={{0,1},{1,2},{2,3},{3,4},{4,5},{5,6},{6,7},{7,8},{8,9},{9,10},{10,1... | collective-permute-start | bytes 30728 | tf_op jit(solution)/shard_map/ppermute | solution.py:19
  778.9 34.8 %collective-permute-start.3 = (f32[2,5,1,256]{3,1,2,0:T(8,128)}, f32[2,5,1,256]{3,1,2,0:T(8,128)}, u32[]{:S(2)}, u32[]{:S(2)}) collective-permute-start(f32[2,5,1,256]{3,1,2,0:T(8,128)} %get-tuple-element.64), channel_id=1, source_target_pairs={{1,0},{2,1},{3,2},{4,3},{5,4},{6,5},{7,6},{8,7},{9,8},{10,9},{11,1... | collective-permute-start | bytes 30728 | tf_op jit(solution)/shard_map/ppermute | solution.py:20
  807.4 1.0 copy-start.2
Sparse Core Ops, SparseCore 0:
  9.8 39.8 all-gather.4
  283.7 30.3 all-gather.6
